TPU v7x, 32 devices: a whole 2x2x4 slice. The times are simulated.
32 devices in a mesh: rep: 2 (over y), grid: 4 (over z), member: 4 (over x, core).
Axes of the slice: x: 2, y: 2, z: 4, core: 2. Of those that a mesh axis runs over, the one named last changes fastest.
Arguments:
- latent: bfloat16 [2, 4, 1024, 2048], P(None, 'member', None, ('rep', 'grid')), parts along dimension 3, may hold values from -6 to 6
- targets: float32 [2, 100, 2048], P(None, None, ('rep', 'grid')), parts along dimension 2, may hold values from -6 to 6
- w1: bfloat16 [768, 1024], P('grid'), may hold values from -0.1875 to 0.1875
- w2: bfloat16 [100, 768], P(None, 'grid'), may hold values from -0.21875 to 0.21875
- noise_table: float32 [4, 768], replicated, may hold values from -6 to 6
- member_ids: int32 [8], P(('rep', 'member')), parts along dimension 0, may hold values from 0 to 3, each once
- lat_weight: float32 [48], replicated, may hold values from 0.1 to 1
- area_index: int32 [2048], P(('rep', 'grid')), parts along dimension 0, may hold values from 0 to 47
- var_weight: float32 [100], replicated, may hold values from 0.2 to 2
Outputs:
- loss: float32 [2], P('rep'), parts along dimension 0
- latent_grad: bfloat16 [2, 4, 1024, 2048], P(None, 'member', None, ('rep', 'grid')), parts along dimension 3
- w1_grad: float32 [1536, 1024], P(('rep', 'grid')), parts along dimension 0
- w2_grad: float32 [100, 1536], P(None, ('rep', 'grid')), parts along dimension 1
There are 2 independent parts, one for each index of `rep`. A program takes and returns all parts, laid end to end along the dimension named above; an argument that names none is the same for every part. Nothing has to cross between parts.
Inputs may be any that keep to these rules, and one draw needn't show every extreme that they name: `member_ids`: each member slot names a different embedding row.
All inputs are finite; a program needn't handle non-finite values.
Results may differ from a plain program's by a relative error of at most 0.011.
The roundings to bfloat16 on the way count: a program that leaves them out, or rounds other values in their place, can miss the bound.
Values may be sent and summed in bfloat16 or wider, within the bound.
A program may use at most 64 MiB of HBM per device.

v0:
```python
import jax
import jax.numpy as jnp
from jax import lax
from jax.sharding import PartitionSpec as P

alpha_fair = 0.95
smooth_width = 0.05
loss_scale = 64.0
grad_shrink = 1.0 / 1024.0


def smooth_abs(diff):
    return jnp.sqrt(diff * diff + smooth_width * smooth_width) - smooth_width


def smooth_sign(diff):
    return diff / jnp.sqrt(diff * diff + smooth_width * smooth_width)


def on_device(latent, targets, w1, w2, noise_table, member_ids, lat_weight, area_index, var_weight):
    members = lax.axis_size("member")
    grid_count = lax.axis_size("grid")
    inputs = latent[:, 0]
    steps = inputs.shape[0]
    points = inputs.shape[2]
    variables = targets.shape[1]
    total_points = points * grid_count
    fairness = (1.0 - alpha_fair) / members
    pair_coef = (1.0 - fairness) / (members * (members - 1))
    lookup = (jnp.arange(lat_weight.shape[0])[:, None] == area_index[None, :]).astype(jnp.float32)
    area = jnp.sum(lookup * lat_weight[:, None], axis=0)
    local_area = jnp.sum(area)
    area_total = lax.psum(local_area, "grid")
    chooser = (jnp.arange(noise_table.shape[0]) == member_ids[0]).astype(jnp.float32)
    noise = jnp.sum(noise_table * chooser[:, None], axis=0)
    before = (
        jnp.einsum(
            "hl,slp->shp",
            lax.all_gather(w1, "grid", axis=0, tiled=True),
            inputs,
            preferred_element_type=jnp.float32,
        )
        + noise[None, :, None]
    )
    hidden = jax.nn.gelu(before).astype(jnp.bfloat16)
    w2_full = lax.all_gather(w2, "grid", axis=1, tiled=True)
    fields = jnp.einsum("vh,shp->svp", w2_full, hidden, preferred_element_type=jnp.float32)
    weight = var_weight[:, None] * area[None, :]
    everyone = lax.all_gather(fields[None], "member", axis=0, tiled=True)
    spread = fields[None] - everyone
    pair_loss = jnp.sum(smooth_abs(spread), axis=0)
    pair_grad = jnp.sum(smooth_sign(spread), axis=0)
    error = fields - targets
    term = smooth_abs(error) / members - 0.5 * pair_coef * pair_loss
    loss_local = jnp.sum(weight[None] * term)
    cotangent = (
        loss_scale * weight[None] * (smooth_sign(error) / members - pair_coef * pair_grad)
    ).astype(jnp.bfloat16)
    back_hidden = jnp.einsum("vh,svp->shp", w2_full, cotangent, preferred_element_type=jnp.float32)
    unused, pullback = jax.vjp(jax.nn.gelu, before)
    back_before = pullback(back_hidden)[0].astype(jnp.bfloat16)
    back_input = jnp.einsum(
        "hl,shp->slp",
        lax.all_gather(w1, "grid", axis=0, tiled=True),
        back_before,
        preferred_element_type=jnp.float32,
    )
    grad_first = jnp.einsum("shp,slp->hl", back_before, inputs, preferred_element_type=jnp.float32)
    grad_second = jnp.einsum("shp,svp->hv", hidden, cotangent, preferred_element_type=jnp.float32)
    grid_sums = (
        lax.psum_scatter(grad_first, "grid", scatter_dimension=0, tiled=True),
        lax.psum_scatter(grad_second, "grid", scatter_dimension=0, tiled=True),
    )
    first_rows, second_rows = lax.psum((grid_sums[0], grid_sums[1]), "member")
    loss_total = lax.psum(loss_local, ("grid", "member"))
    scale = total_points / area_total
    latent_grad = (back_input * scale).astype(jnp.bfloat16)[:, None]
    w1_grad = first_rows * (scale * grad_shrink)
    w2_grad = jnp.transpose(second_rows) * (scale * grad_shrink)
    loss = jnp.reshape(loss_total / (area_total * steps * variables), (1,))
    return (loss, latent_grad, w1_grad, w2_grad)


def solution(mesh):
    return jax.shard_map(
        on_device,
        mesh=mesh,
        in_specs=(
            P(None, "member", None, ("rep", "grid")),
            P(None, None, ("rep", "grid")),
            P("grid", None),
            P(None, "grid"),
            P(),
            P(("rep", "member")),
            P(),
            P(("rep", "grid")),
            P(),
        ),
        out_specs=(
            P("rep"),
            P(None, "member", None, ("rep", "grid")),
            P(("rep", "grid"), None),
            P(None, ("rep", "grid")),
        ),
        check_vma=False,
    )
```

profile of v0, /device:TPU:0, one launch (start us, length us, event | category | flops | bytes accessed | tf_op | source)
XLA Modules:
  0.0 203.5 jit_solution(12443616244400026623)
XLA Ops:
  7.2 0.0 copy-start
  7.2 0.0 all-gather.3.cloned.1.call-start
  7.2 0.7 all-gather.3.cloned.1.call-update
  7.9 0.0 reduce-scatter.5.cloned.1.call-start
  8.6 15.8 %all_gather.11 = bf16[100,768]{0,1:T(8,128)(2,1)S(1)} all-gather(bf16[100,192]{0,1:T(8,128)(2,1)} %param.12), channel_id=1, replica_groups=mesh['rep'=2,'grid'=4,'member'=4] {'grid'}, dimensions={1}, use_global_device_ids=true | all-gather | bytes 192000 | tf_op jit(solution)/shard_map/all_gather | solution.py:46
  24.4 0.8 multiply_reduce_fusion.1
  25.2 1.4 select_reduce_fusion
  26.6 0.7 broadcast_multiply_fusion.1
  27.3 22.6 %all-gather.3.cloned.1.call-done = bf16[768,1024]{1,0:T(8,128)(2,1)} async-done(((bf16[192,1024]{1,0:T(8,128)(2,1)}), bf16[768,1024]{1,0:T(8,128)(2,1)}) %all-gather.3.cloned.1.call-update) | async-done | bytes 1572880 | tf_op jit(solution)/shard_map/all_gather | solution.py:39
  49.9 0.0 copy-done
  49.9 3.9 %fusion.10 = (bf16[2,768,256]{1,2,0:T(8,128)(2,1)S(1)}, f32[2,256,768]{2,1,0:T(8,128)}) fusion(f32[768]{0:T(1024)S(1)} %multiply_reduce_fusion.1, bf16[768,1024]{1,0:T(8,128)(2,1)} %all-gather.3.cloned.1.call-done, bf16[2,1,1024,256]{3,2,1,0:T(8,128)(2,1)S(1)} %copy-done), kind=kOutput, calls=%fused_computation.17 | convolution fusion | flops 809238528 | bytes 4983808 | tf_op jit(solution)/shard_map/hl,slp->shp/dot_general | solution.py:37
  53.8 0.4 convolution_bitcast_fusion.2
  54.1 0.0 copy-start.1
  54.2 9.1 %all-gather = f32[8,100,256]{2,1,0:T(8,128)S(1)} all-gather(f32[2,100,256]{2,1,0:T(8,128)S(1)} %convolution_bitcast_fusion.2), channel_id=2, replica_groups=mesh['rep'=2,'grid'=4,'member'=4] {'member'}, dimensions={0}, use_global_device_ids=true | all-gather | bytes 1024000 | tf_op jit(solution)/shard_map/all_gather | solution.py:49
  63.2 0.5 divide_reduce_fusion
  63.7 0.0 copy-done.1
  63.7 0.8 multiply_convert_fusion.1
  64.5 1.2 convolution_bitcast_fusion.1
  65.7 0.0 reduce-scatter.5.cloned.1.call-update
  65.7 0.0 reduce-scatter.3.cloned.1.call-start
  65.7 2.6 %fusion.6 = bf16[2,768,256]{1,2,0:T(8,128)(2,1)S(1)} fusion(f32[2,256,768]{2,1,0:T(8,128)} %get-tuple-element.27, bf16[2,100,256]{2,1,0:T(8,128)(2,1)S(1)} %get-tuple-element.22, bf16[100,768]{0,1:T(8,128)(2,1)S(1)} %all_gather.11), kind=kOutput, calls=%fused_computation.10 | convolution fusion | flops 86507520 | bytes 2615296 | tf_op jit(solution)/shard_map/vh,svp->shp/dot_general | solution.py:59
  68.4 2.7 %convolution_bitcast_fusion = f32[768,1024]{1,0:T(8,128)} fusion(bf16[2,768,256]{1,2,0:T(8,128)(2,1)S(1)} %fusion.6, bf16[2,1,1024,256]{3,2,1,0:T(8,128)(2,1)S(1)} %copy-done), kind=kOutput, calls=%fused_computation.3 | convolution fusion | flops 805306368 | bytes 4980736 | tf_op jit(solution)/shard_map/shp,slp->hl/dot_general | solution.py:68
  71.1 0.0 reduce-scatter.3.cloned.1.call-update
  71.1 0.0 all-reduce.3.cloned.1.call-start
  71.1 13.8 %reduce-scatter.5.cloned.1.call-done = f32[192,100]{1,0:T(8,128)} async-done(((f32[768,100]{1,0:T(8,128)}), f32[192,100]{1,0:T(8,128)}) %reduce-scatter.5.cloned.1.call-update) | async-done | bytes 76816 | tf_op jit(solution)/shard_map/reduce_scatter | solution.py:72
  84.9 61.0 %reduce-scatter.3.cloned.1.call-done = f32[192,1024]{1,0:T(8,128)} async-done(((f32[768,1024]{1,0:T(8,128)}), f32[192,1024]{1,0:T(8,128)}) %reduce-scatter.3.cloned.1.call-update) | async-done | bytes 786448 | tf_op jit(solution)/shard_map/reduce_scatter | solution.py:71
  145.9 0.0 all-reduce.3.cloned.1.call-update
  145.9 11.1 %psum.29 = f32[]{:T(128)} all-reduce(f32[]{:T(128)} %get-tuple-element.18), channel_id=1, replica_groups=mesh['rep'=2,'grid'=4,'member'=4] {'grid'}, use_global_device_ids=true, to_apply=%region_6.0 | all-reduce | flops 1 | bytes 8 | tf_op jit(solution)/shard_map/psum | solution.py:33
  158.4 30.3 %psum.28 = f32[]{:T(128)} all-reduce(f32[]{:T(128)} %get-tuple-element.23), channel_id=1, replica_groups=mesh['rep'=2,'grid'=4,'member'=4] {'grid','member'}, use_global_device_ids=true, to_apply=%region_4.0 | all-reduce | flops 1 | bytes 8 | tf_op jit(solution)/shard_map/psum | solution.py:75
  188.7 2.4 %fusion.17 = bf16[2,1,1024,256]{2,3,0,1:T(8,128)(2,1)S(1)} fusion(bf16[2,768,256]{1,2,0:T(8,128)(2,1)S(1)} %fusion.6, bf16[768,1024]{1,0:T(8,128)(2,1)} %all-gather.3.cloned.1.call-done, f32[]{:T(128)S(6)} %div.23), kind=kOutput, calls=%fused_computation.22 | convolution fusion | flops 806354944 | bytes 3407876 | tf_op jit(solution)/shard_map/hl,shp->slp/dot_general | solution.py:62
  191.1 1.3 copy.30
  193.0 0.0 all-reduce.3.cloned.1.call-done
  193.1 0.0 copy-start.2
  193.1 2.1 %broadcast_multiply_fusion = f32[192,1024]{1,0:T(8,128)} fusion(f32[192,1024]{1,0:T(8,128)} %get-tuple-element.20, f32[]{:T(128)S(6)} %mul.197), kind=kLoop, calls=%fused_computation.30 | loop fusion | flops 196608 | bytes 1572868 | tf_op jit(solution)/shard_map/mul | solution.py:78
  195.2 0.0 copy-done.2
  195.2 0.6 multiply_bitcast_fusion
  (1 shorter events, 0.0 us)
Async XLA Ops:
  7.2 42.7 %copy-start = (bf16[2,1,1024,256]{3,2,1,0:T(8,128)(2,1)S(1)}, bf16[2,1,1024,256]{3,2,1,0:T(8,128)(2,1)}, u32[]{:S(2)}) copy-start(bf16[2,1,1024,256]{3,2,1,0:T(8,128)(2,1)} %param.9) | copy-start | bytes 3145732
  7.2 42.7 %all-gather.3.cloned.1.call-start = ((), (), s32[]{:S(2)}) async-start(), calls=%async_computation.2 | async-start | bytes 1966080 | tf_op jit(solution)/shard_map/all_gather | solution.py:39
  7.9 77.0 %reduce-scatter.5.cloned.1.call-start = ((), (), s32[]{:S(2)}) async-start(), calls=%async_computation.4 | async-start | bytes 491520 | tf_op jit(solution)/shard_map/reduce_scatter | solution.py:72
  54.1 9.6 %copy-start.1 = (f32[2,100,256]{2,0,1:T(2,128)S(1)}, f32[2,100,256]{2,0,1:T(2,128)}, u32[]{:S(2)}) copy-start(f32[2,100,256]{2,0,1:T(2,128)} %param.10) | copy-start | bytes 614404
  65.7 80.2 %reduce-scatter.3.cloned.1.call-start = ((), (), s32[]{:S(2)}) async-start(), calls=%async_computation.3 | async-start | bytes 3932160 | tf_op jit(solution)/shard_map/reduce_scatter | solution.py:71
  71.1 122.0 %all-reduce.3.cloned.1.call-start = ((), (), s32[]{:S(2)}) async-start(), calls=%async_computation.5 | async-start | bytes 1769472 | tf_op jit(solution)/shard_map/psum | solution.py:74
  193.1 2.1 %copy-start.2 = (f32[192,100]{1,0:T(8,128)S(1)}, f32[192,100]{1,0:T(8,128)}, u32[]{:S(2)}) copy-start(f32[192,100]{1,0:T(8,128)} %get-tuple-element.21) | copy-start | bytes 230404
Sparse Core Ops, SparseCore 0:
  9.6 40.2 all-gather.2
  65.8 19.0 reduce-scatter.4
  87.3 58.5 reduce-scatter.2
  148.4 35.3 all-reduce.2
where the time goes:
time: 204 us
  waiting for transfers between devices  98.1 us (48%)
  blocking collectives  66.3 us (32%)
  between operations  17.6 us (9%)
  matrix products  13.1 us (6%)
  other arithmetic  6.96 us (3%)
    reduce_scatter x1, waiting for transfers between devices, on_device(): lax.psum_scatter(grad_first, 'grid', scatter_dimension=0, tiled=True)  61 us
    psum x1, blocking collectives, on_device(): loss_total = lax.psum(loss_local, ('grid', 'member'))  30.3 us
    all_gather x1, waiting for transfers between devices, on_device(): lax.all_gather(w1, 'grid', axis=0, tiled=True)  22.6 us
    all_gather x1, blocking collectives, on_device(): w2_full = lax.all_gather(w2, 'grid', axis=1, tiled=True)  15.8 us
    reduce_scatter x1, waiting for transfers between devices, on_device(): lax.psum_scatter(grad_second, 'grid', scatter_dimension=0, tiled=True)  13.8 us
    psum x1, blocking collectives, on_device(): area_total = lax.psum(local_area, 'grid')  11.1 us
    all_gather x1, blocking collectives, on_device(): everyone = lax.all_gather(fields[None], 'member', axis=0, tiled=True)  9.06 us
  transfers between devices with their start and end apart: 4, of which 3 were waited for; matrix products, arithmetic and copies ran while one was open for 6% of the time, Pallas kernels for 0%

commit v1 on v0

--- a/solution.py
+++ b/solution.py
@@ -1,6 +1,11 @@
+import functools
+import math
+
 import jax
 import jax.numpy as jnp
 from jax import lax
+from jax.experimental import pallas as pl
+from jax.experimental.pallas import tpu as pltpu
 from jax.sharding import PartitionSpec as P
 
 alpha_fair = 0.95
@@ -81,9 +86,379 @@
     return (loss, latent_grad, w1_grad, w2_grad)
 
 
+MESH = pl.DeviceIdType.MESH
+GRID = 4
+MEMB = 4
+TANH_SCALE = math.sqrt(2.0 / math.pi)
+CUBIC = 0.044715
+
+
+def gelu_and_slope(x):
+    square = x * x
+    t = jnp.tanh(TANH_SCALE * x * (1.0 + CUBIC * square))
+    half = 0.5 * (1.0 + t)
+    slope = half + 0.5 * x * (1.0 - t * t) * (TANH_SCALE * (1.0 + 3.0 * CUBIC * square))
+    return x * half, slope
+
+
+def pick(index, values):
+    result = values[-1]
+    for i in range(len(values) - 1):
+        result = jnp.where(index == i, values[i], result)
+    return result
+
+
+def dot(a, b, contract):
+    return lax.dot_general(a, b, ((contract[:1], contract[1:]), ((), ())), preferred_element_type=jnp.float32)
+
+
+class Slots:
+    def __init__(self):
+        self.count = 0
+
+    def take(self, n=1):
+        self.count += n
+        return self.count - n
+
+
+SEM = Slots()
+AREA, W_RECV, W_LEFT, W_CORE = SEM.take(4), SEM.take(4), SEM.take(1), SEM.take(4)
+F_CORE, F_X, F_DIAG = SEM.take(2), SEM.take(2), SEM.take(2)
+G_CORE, G_ZR, G_ZL, G_X, G_FIN = SEM.take(4), SEM.take(4), SEM.take(4), SEM.take(1), SEM.take(1)
+L_MEM, L_GRID = SEM.take(4), SEM.take(4)
+
+
+def fused(
+    lat_hbm, tgt_hbm, w1_hbm, w2_ref, table_ref, ids_ref, latw_ref, aidx_ref, vw_ref,
+    loss_ref, lg_hbm, w1g_hbm, w2g_ref,
+    lat, tgt, wx, noise, slope, hid, fall, cot, bb, acc, csend, crecv, zsend, zin, xsend, xrecv, fin, lgv, pad,
+    abuf, lmem, lgrid, ss, rs, ls,
+):
+    g, m = lax.axis_index("grid"), lax.axis_index("member")
+    c = lax.rem(m, 2)
+    core_peer, x_peer = m + 1 - 2 * c, lax.rem(m + 2, 4)
+    diag_peer = lax.rem(core_peer + 2, 4)
+    steps, _, feats, points = lat_hbm.shape
+    variables = tgt_hbm.shape[1]
+    rows = w1_hbm.shape[0]
+    half = rows // 2
+    fairness = (1.0 - alpha_fair) / MEMB
+    pair_coef = (1.0 - fairness) / (MEMB * (MEMB - 1))
+
+    def block(t):
+        return pl.ds(pl.multiple_of(t * rows, rows), rows)
+
+    def half_of(t, which):
+        return pl.ds(pl.multiple_of(t * rows + which * half, half), half)
+
+    def send(src, dst, s_index, r_index, **where):
+        return pltpu.make_async_remote_copy(
+            src_ref=src, dst_ref=dst, send_sem=ss.at[s_index], recv_sem=rs.at[r_index],
+            device_id={"grid": where.get("grid", g), "member": where.get("member", m), "rep": lax.axis_index("rep")},
+            device_id_type=MESH,
+        )
+
+    w1_in = pltpu.make_async_copy(w1_hbm, wx.at[block(g), pl.ds(0, feats)], ls.at[0])
+    w1_in.start()
+    lat_in = pltpu.make_async_copy(lat_hbm.at[:, 0], lat, ls.at[1])
+    lat_in.start()
+    tgt_in = pltpu.make_async_copy(tgt_hbm, tgt, ls.at[2])
+    tgt_in.start()
+
+    barrier = pltpu.get_barrier_semaphore()
+    for k in range(1, 4):
+        pl.semaphore_signal(barrier, inc=1, device_id={"grid": lax.rem(g + k, 4), "member": m, "rep": lax.axis_index("rep")}, device_id_type=MESH)
+        pl.semaphore_signal(barrier, inc=1, device_id={"grid": g, "member": lax.rem(m + k, 4), "rep": lax.axis_index("rep")}, device_id_type=MESH)
+
+    pad[...] = jnp.zeros_like(pad)
+    pad[:variables, :rows] = w2_ref[...].astype(jnp.float32)
+    wx[block(g), feats:] = jnp.transpose(pad[...])[:rows].astype(jnp.bfloat16)
+    w1_in.wait()
+    pl.semaphore_wait(barrier, 6)
+
+    own_half = half_of(g, c)
+    own_right = send(wx.at[own_half], wx.at[own_half], W_RECV + g, W_RECV + g, grid=jnp.minimum(g + 1, 3))
+    own_left = send(wx.at[own_half], wx.at[own_half], W_LEFT, W_RECV + g, grid=jnp.maximum(g - 1, 0))
+    pl.when(g < 3)(own_right.start)
+    pl.when(g > 0)(own_left.start)
+
+    n_lat = latw_ref.shape[1]
+    diagonal = lax.broadcasted_iota(jnp.int32, (n_lat, n_lat), 0) == lax.broadcasted_iota(jnp.int32, (n_lat, n_lat), 1)
+    lat_col = jnp.sum(jnp.where(diagonal, latw_ref[...], 0.0), axis=1, keepdims=True)
+    lookup = lax.broadcasted_iota(jnp.int32, (n_lat, points), 0) == aidx_ref[...]
+    area = jnp.sum(jnp.where(lookup, lat_col, 0.0), axis=0, keepdims=True)
+    abuf[pl.ds(g, 1)] = jnp.full((1, 8, 128), jnp.sum(area), jnp.float32)
+    area_sends = [
+        send(abuf.at[g], abuf.at[g], AREA + k, AREA + g, grid=lax.rem(g + k, 4)) for k in range(1, 4)
+    ]
+    for copy in area_sends:
+        copy.start()
+    diagonal = lax.broadcasted_iota(jnp.int32, (variables, variables), 0) == lax.broadcasted_iota(jnp.int32, (variables, variables), 1)
+    var_col = jnp.sum(jnp.where(diagonal, vw_ref[...], 0.0), axis=1, keepdims=True)
+    weight = var_col * area
+
+    chosen = lax.broadcasted_iota(jnp.int32, table_ref.shape, 0) == ids_ref[0]
+    noise_row = jnp.sum(jnp.where(chosen, table_ref[...], 0.0), axis=0, keepdims=True)
+    noise[...] = jnp.transpose(jnp.broadcast_to(noise_row, (128, noise_row.shape[1])))
+    cot[...] = jnp.zeros_like(cot)
+    lat_in.wait()
+
+    fields = [None] * steps
+    field_sends = []
+    mirrored = g >= 2
+    near = jnp.where(mirrored, 3 - g, g)
+    w_sends = []
+    for j in range(GRID):
+        o = pick(near, (j, (1, 0, 2, 3)[j]))
+        o = jnp.where(mirrored, 3 - o, o)
+        if j > 0:
+            mine, other = half_of(o, c), half_of(o, 1 - c)
+            send(wx.at[mine], wx.at[mine], W_RECV + o, W_RECV + o).wait_recv()
+            to_core = send(wx.at[mine], wx.at[mine], W_CORE + o, W_CORE + o, member=core_peer)
+            to_core.start()
+            ahead = jnp.where(o < g, g + 1, g - 1)
+            valid = jnp.logical_and(ahead >= 0, ahead < GRID)
+            onward = send(wx.at[mine], wx.at[mine], W_RECV + o, W_RECV + o, grid=jnp.clip(ahead, 0, 3))
+            pl.when(valid)(onward.start)
+            w_sends.append((to_core, onward, valid))
+            send(wx.at[other], wx.at[other], W_CORE + o, W_CORE + o).wait_recv()
+        shift = noise[block(o), :]
+        shift = jnp.concatenate([shift] * (points // 128), axis=1)
+        for s in range(steps):
+            before = dot(wx[block(o), :feats], lat[s], (1, 0)) + shift
+            value, grad = gelu_and_slope(before)
+            value = value.astype(jnp.bfloat16)
+            cols = slice(s * points, (s + 1) * points)
+            slope[block(o), cols] = grad
+            hid[block(o), cols] = value
+            part = dot(wx[block(o), feats:], value, (0, 0))
+            fields[s] = part if j == 0 else fields[s] + part
+            if j == GRID - 1:
+                fall[pl.ds(m, 1), s] = fields[s][None, : fall.shape[2]]
+                mine = fall.at[m, s]
+                pair = (
+                    send(mine, mine, F_X + s, F_X + s, member=x_peer),
+                    send(mine, mine, F_CORE + s, F_CORE + s, member=core_peer),
+                )
+                for copy in pair:
+                    copy.start()
+                field_sends.extend(pair)
+
+    tgt_in.wait()
+    for k in range(1, 4):
+        o = lax.rem(g + k, 4)
+        send(abuf.at[o], abuf.at[o], AREA + k, AREA + o).wait_recv()
+    area_total = abuf[0] + abuf[1] + abuf[2] + abuf[3]
+    area_total = area_total[:1, :1]
+    scale = (points * GRID) / area_total
+
+    for s in range(steps):
+        theirs = fall.at[x_peer, s]
+        send(theirs, theirs, F_X + s, F_X + s).wait_recv()
+        onward = send(theirs, theirs, F_DIAG + s, F_DIAG + s, member=core_peer)
+        onward.start()
+        field_sends.append(onward)
+    loss_sum = jnp.zeros((1, 1), jnp.float32)
+    for s in range(steps):
+        cols = slice(s * points, (s + 1) * points)
+        own = fields[s][:variables]
+        error = own - tgt[s]
+        root = jnp.sqrt(error * error + smooth_width * smooth_width)
+        term = (root - smooth_width) / MEMB
+        grad = error / root / MEMB
+        near_ref = fall.at[core_peer, s]
+        send(near_ref, near_ref, F_CORE + s, F_CORE + s).wait_recv()
+        far_ref = fall.at[diag_peer, s]
+        for peer in (x_peer, core_peer, diag_peer):
+            if peer is diag_peer:
+                send(far_ref, far_ref, F_DIAG + s, F_DIAG + s).wait_recv()
+            spread = own - fall[pl.ds(peer, 1), s][0, :variables]
+            root = jnp.sqrt(spread * spread + smooth_width * smooth_width)
+            term = term - (0.5 * pair_coef) * (root - smooth_width)
+            grad = grad - pair_coef * (spread / root)
+        loss_sum = loss_sum + jnp.sum(weight * term)
+        cot[:variables, cols] = (loss_scale * weight * grad).astype(jnp.bfloat16)
+        bb[:, cols] = (dot(wx[:, feats:], cot[:, cols], (1, 0)) * slope[:, cols]).astype(jnp.bfloat16)
+
+    lmem[pl.ds(m, 1)] = jnp.broadcast_to(loss_sum, (1, 8, 128))
+    late = [send(lmem.at[m], lmem.at[m], L_MEM + k, L_MEM + m, member=lax.rem(m + k, 4)) for k in range(1, 4)]
+    for copy in late:
+        copy.start()
+
+    order = [
+        pick(g, (3, 3, 0, 0)),
+        pick(g, (2, 0, 3, 1)),
+        pick(g, (1, 2, 1, 2)),
+        g,
+    ]
+    for j, t in enumerate(order):
+        first = dot(bb[block(t), :points], lat[0], (1, 1))
+        for s in range(1, steps):
+            first = first + dot(bb[block(t), s * points : (s + 1) * points], lat[s], (1, 1))
+        second = dot(hid[block(t), :], cot[...], (1, 1))
+        for which in range(2):
+            part = slice(which * half, (which + 1) * half)
+
+            @pl.when(c == which)
+            def _():
+                acc[j, :, :feats] = first[part]
+                acc[j, :, feats:] = second[part]
+
+            @pl.when(c != which)
+            def _():
+                csend[j, :, :feats] = first[part].astype(jnp.bfloat16)
+                csend[j, :, feats:] = second[part].astype(jnp.bfloat16)
+
+        copy = send(csend.at[j], crecv.at[j], G_CORE + j, G_CORE + j, member=core_peer)
+        copy.start()
+        late.append(copy)
+
+    def back_input(s, piece):
+        cols = slice(s * points, (s + 1) * points)
+        span = slice(piece * 256, (piece + 1) * 256)
+        lgv[s, span] = (dot(wx[:, span], bb[:, cols], (0, 0)) * scale).astype(jnp.bfloat16)
+
+    pieces = [(s, p) for s in range(steps) for p in range(feats // 256)]
+    share = -(-len(pieces) // 3)
+    z_sends = []
+    for j, t in enumerate(order):
+        send(csend.at[j], crecv.at[j], G_CORE + j, G_CORE + j).wait_recv()
+        total = acc[j] + crecv[j].astype(jnp.float32)
+        from_left = jnp.logical_and(g > 0, t >= g)
+        from_right = jnp.logical_and(g < 3, t <= g)
+        acc[j] = total
+        for present, base, side in ((from_left, G_ZR, 0), (from_right, G_ZL, 1)):
+
+            @pl.when(present)
+            def _():
+                send(zin.at[side, t], zin.at[side, t], base + t, base + t).wait_recv()
+                acc[j] = acc[j] + zin[side, pl.ds(t, 1)][0].astype(jnp.float32)
+
+        if j < GRID - 1:
+            zsend[j] = acc[j].astype(jnp.bfloat16)
+            right = send(zsend.at[j], zin.at[0, t], G_ZR + j, G_ZR + t, grid=jnp.minimum(g + 1, 3))
+            left = send(zsend.at[j], zin.at[1, t], G_ZL + j, G_ZL + t, grid=jnp.maximum(g - 1, 0))
+            pl.when(t > g)(right.start)
+            pl.when(t < g)(left.start)
+            z_sends.append((right, t > g, left, t < g))
+            for s, p in pieces[j * share : (j + 1) * share]:
+                back_input(s, p)
+            if j == 0:
+                for k in range(1, 4):
+                    o = lax.rem(m + k, 4)
+                    send(lmem.at[o], lmem.at[o], L_MEM + k, L_MEM + o).wait_recv()
+                lgrid[pl.ds(g, 1)] = (lmem[0] + lmem[1] + lmem[2] + lmem[3])[None]
+                for k in range(1, 4):
+                    copy = send(lgrid.at[g], lgrid.at[g], L_GRID + k, L_GRID + g, grid=lax.rem(g + k, 4))
+                    copy.start()
+                    late.append(copy)
+            if j == GRID - 2:
+                lg_out = pltpu.make_async_copy(lgv, lg_hbm.at[:, 0], ls.at[3])
+                lg_out.start()
+                for k in range(1, 4):
+                    o = lax.rem(g + k, 4)
+                    send(lgrid.at[o], lgrid.at[o], L_GRID + k, L_GRID + o).wait_recv()
+                loss_total = lgrid[0] + lgrid[1] + lgrid[2] + lgrid[3]
+                loss_ref[...] = loss_total[:1, :1] / (area_total * (steps * variables))
+
+    xsend[...] = acc[GRID - 1].astype(jnp.bfloat16)
+    copy = send(xsend, xrecv, G_X, G_X, member=x_peer)
+    copy.start()
+    late.append(copy)
+    copy.wait_recv()
+    mine, other = half_of(0, c), half_of(0, 1 - c)
+    fin[mine] = (xsend[...].astype(jnp.float32) + xrecv[...].astype(jnp.float32)) * (scale * grad_shrink)
+    copy = send(fin.at[mine], fin.at[mine], G_FIN, G_FIN, member=core_peer)
+    copy.start()
+    mine_out = pltpu.make_async_copy(fin.at[mine, pl.ds(0, feats)], w1g_hbm.at[mine], ls.at[4])
+    mine_out.start()
+    send(fin.at[other], fin.at[other], G_FIN, G_FIN).wait_recv()
+    other_out = pltpu.make_async_copy(fin.at[other, pl.ds(0, feats)], w1g_hbm.at[other], ls.at[5])
+    other_out.start()
+    pad[:, :rows] = jnp.transpose(
+        jnp.concatenate([fin[:, feats:], jnp.zeros((pad.shape[1] - rows, 128), jnp.float32)], axis=0)
+    )[:, :rows]
+    w2g_ref[...] = pad[:variables, :rows]
+
+    pl.when(g < 3)(own_right.wait_send)
+    pl.when(g > 0)(own_left.wait_send)
+    for to_core, onward, valid in w_sends:
+        to_core.wait_send()
+        pl.when(valid)(onward.wait_send)
+    for copy in area_sends + field_sends + late + [copy]:
+        copy.wait_send()
+    for right, go_right, left, go_left in z_sends:
+        pl.when(go_right)(right.wait_send)
+        pl.when(go_left)(left.wait_send)
+    lg_out.wait()
+    mine_out.wait()
+    other_out.wait()
+
+
+def fused_on_device(latent, targets, w1, w2, noise_table, member_ids, lat_weight, area_index, var_weight):
+    steps, _, feats, points = latent.shape
+    variables = targets.shape[1]
+    rows = w1.shape[0]
+    hidden = rows * GRID
+    half = rows // 2
+    wide = feats + 128
+    padded = -(-variables // 8) * 8
+    f32, bf16 = jnp.float32, jnp.bfloat16
+    hbm, vmem = pl.BlockSpec(memory_space=pl.ANY), pl.BlockSpec(memory_space=pltpu.VMEM)
+    smem = pl.BlockSpec(memory_space=pltpu.SMEM)
+    loss, latent_grad, w1_grad, w2_grad = pl.pallas_call(
+        fused,
+        out_shape=(
+            jax.ShapeDtypeStruct((1, 1), f32),
+            jax.ShapeDtypeStruct(latent.shape, bf16),
+            jax.ShapeDtypeStruct((rows, feats), f32),
+            jax.ShapeDtypeStruct((variables, rows), f32),
+        ),
+        in_specs=[hbm, hbm, hbm, vmem, vmem, smem, vmem, vmem, vmem],
+        out_specs=(vmem, hbm, hbm, vmem),
+        scratch_shapes=[
+            pltpu.VMEM((steps, feats, points), bf16),
+            pltpu.VMEM((steps, variables, points), f32),
+            pltpu.VMEM((hidden, wide), bf16),
+            pltpu.VMEM((hidden, 128), f32),
+            pltpu.VMEM((hidden, steps * points), f32),
+            pltpu.VMEM((hidden, steps * points), bf16),
+            pltpu.VMEM((MEMB, steps, padded, points), f32),
+            pltpu.VMEM((128, steps * points), bf16),
+            pltpu.VMEM((hidden, steps * points), bf16),
+            pltpu.VMEM((GRID, half, wide), f32),
+            pltpu.VMEM((GRID, half, wide), bf16),
+            pltpu.VMEM((GRID, half, wide), bf16),
+            pltpu.VMEM((GRID - 1, half, wide), bf16),
+            pltpu.VMEM((2, GRID, half, wide), bf16),
+            pltpu.VMEM((half, wide), bf16),
+            pltpu.VMEM((half, wide), bf16),
+            pltpu.VMEM((rows, wide), f32),
+            pltpu.VMEM((steps, feats, points), bf16),
+            pltpu.VMEM((128, 256), f32),
+            pltpu.VMEM((GRID, 8, 128), f32),
+            pltpu.VMEM((MEMB, 8, 128), f32),
+            pltpu.VMEM((GRID, 8, 128), f32),
+            pltpu.SemaphoreType.DMA((SEM.count,)),
+            pltpu.SemaphoreType.DMA((SEM.count,)),
+            pltpu.SemaphoreType.DMA((6,)),
+        ],
+        compiler_params=pltpu.CompilerParams(
+            collective_id=0, has_side_effects=True, vmem_limit_bytes=48 * 1024 * 1024
+        ),
+        cost_estimate=pl.CostEstimate(
+            flops=6 * hidden * feats * steps * points, bytes_accessed=4 * 1024 * 1024, transcendentals=hidden * steps * points
+        ),
+    )(
+        latent, targets, w1, w2, noise_table, member_ids,
+        lat_weight[None, :], area_index[None, :], var_weight[None, :],
+    )
+    return jnp.reshape(loss, (1,)), latent_grad, w1_grad, w2_grad
+
+
 def solution(mesh):
     return jax.shard_map(
-        on_device,
+        on_device if tuple(mesh.shape[a] for a in ("grid", "member")) != (4, 4) else fused_on_device,
         mesh=mesh,
         in_specs=(
             P(None, "member", None, ("rep", "grid")),

time: 204 us -> 73.8 us (0.36)
  waiting for transfers between devices: 98.1 us -> 0 us
  blocking collectives: 66.3 us -> 0 us
  Pallas kernels: 0 us -> 64.5 us
  between operations: 17.6 us -> 3.25 us
  matrix products: 13.1 us -> 0 us
  other arithmetic: 6.96 us -> 0 us
  local copies, waits for them, and re-layouts: 1.33 us -> 5.73 us
    reduce_scatter x2 -> x0, waiting for transfers between devices: 74.7 us -> none  [the longest x1 61 us: on_device(): lax.psum_scatter(grad_first, 'grid', scatter_dimension=0, tiled=True)]
    pallas_call x0 -> x1, Pallas kernels: none -> 64.5 us  [fused_on_device(): pl.pallas_call(fused, out_shape=(jax.ShapeDtypeStruct((1, 1), f32), jax.S...]
    psum x2 -> x0, blocking collectives: 41.4 us -> none  [the longest x1 30.3 us: on_device(): loss_total = lax.psum(loss_local, ('grid', 'member'))]
    all_gather x2 -> x0, blocking collectives: 24.8 us -> none  [the longest x1 15.8 us: on_device(): w2_full = lax.all_gather(w2, 'grid', axis=1, tiled=True)]
    all_gather x1 -> x0, waiting for transfers between devices: 22.6 us -> none  [on_device(): lax.all_gather(w1, 'grid', axis=0, tiled=True)]
    dot_general x6 -> x0, matrix products: 13.1 us -> none  [the longest x1 3.9 us: on_device(): jnp.einsum('hl,slp->shp', lax.all_gather(w1, 'grid', axis=0, tiled=True),...]
    unnamed x7 -> x17, local copies, waits for them, and re-layouts: 1.33 us -> 5.73 us
    mul x3 -> x0, other arithmetic: 3.52 us -> none  [the longest x1 2.14 us: on_device(): w1_grad = first_rows * (scale * grad_shrink)]
  transfers between devices with their start and end apart: 4 -> 0, of which waited for: 3 -> 0; matrix products, arithmetic and copies ran while one was open for 6% -> 0% of each run, Pallas kernels for 0% -> 0%
where the time goes in v1:
time: 73.8 us; the launch traced here: 73.5 us
  Pallas kernels  64.5 us (87%)
  local copies, waits for them, and re-layouts  5.73 us (8%)
  between operations  3.25 us (4%)
    pallas_call x1, Pallas kernels, fused_on_device(): pl.pallas_call(fused, out_shape=(jax.ShapeDtypeStruct((1, 1), f32), jax.S...  64.5 us
    unnamed x17, local copies, waits for them, and re-layouts  5.73 us

profile of v1, /device:TPU:0, one launch (start us, length us, event | category | flops | bytes accessed | tf_op | source)
XLA Modules:
  0.0 73.5 jit_solution(2187961019455740883)
XLA Ops:
  0.6 0.0 copy-start.1
  1.3 0.9 %copy.14.w2_ref = bf16[100,192]{1,0:T(8,128)(2,1)S(1)} copy(bf16[100,192]{0,1:T(8,128)(2,1)} %param.12) | data formatting | bytes 76800 | tf_op args[3]
  2.2 0.0 copy-start.2
  2.3 0.0 copy-start.3
  2.3 0.0 copy-start.4
  2.3 0.0 copy-start.5
  2.3 1.0 %copy.13.tgt_hbm = f32[2,100,256]{2,1,0:T(8,128)S(1)} copy(f32[2,100,256]{2,0,1:T(2,128)} %param.10) | data formatting | bytes 409600 | tf_op args[1]
  3.3 0.0 copy-done.1
  3.3 0.0 copy-done.2
  3.3 0.0 copy-done.3
  3.3 0.0 copy-done.4
  3.3 0.0 copy-done.5
  3.3 0.0 copy-start
  3.3 1.2 %copy-done = bf16[2,1,1024,256]{3,2,1,0:T(8,128)(2,1)S(1)} copy-done((bf16[2,1,1024,256]{3,2,1,0:T(8,128)(2,1)S(1)}, bf16[2,1,1024,256]{3,2,1,0:T(8,128)(2,1)}, u32[]{:S(2)}) %copy-start) | copy-done | bytes 1048600
  4.5 64.5 %shard_map.120 = (f32[1,1]{1,0:T(1,128)}, bf16[2,1,1024,256]{3,2,1,0:T(8,128)(2,1)S(1)}, f32[192,1024]{1,0:T(8,128)S(1)}, f32[100,192]{1,0:T(8,128)S(1)}) custom-call(bf16[2,1,1024,256]{3,2,1,0:T(8,128)(2,1)S(1)} %copy-done, f32[2,100,256]{2,1,0:T(8,128)S(1)} %copy.13.tgt_hbm, bf16[192,1024]{1,0:T(8,128)(2,1)S(1)} %copy-done.1, ...), custom_call_target="tpu_custom_call" | custom-call | flops 2415919104 | bytes 4194304 | tf_op jit(solution)/shard_map/pallas_call | solution.py:409
  69.1 0.7 %copy.15 = f32[100,192]{0,1:T(8,128)} copy(f32[100,192]{1,0:T(8,128)S(1)} %get-tuple-element.15) | data formatting | bytes 153600
  70.5 1.0 %copy.21 = bf16[2,1,1024,256]{3,2,1,0:T(8,128)(2,1)} copy(bf16[2,1,1024,256]{3,2,1,0:T(8,128)(2,1)S(1)} %get-tuple-element.21) | data formatting | bytes 2097152
  71.5 0.9 %copy.22 = f32[192,1024]{1,0:T(8,128)} copy(f32[192,1024]{1,0:T(8,128)S(1)} %get-tuple-element.22) | data formatting | bytes 1572864
Async XLA Ops:
  0.6 2.6 %copy-start.1 = (bf16[192,1024]{1,0:T(8,128)(2,1)S(1)}, bf16[192,1024]{1,0:T(8,128)(2,1)}, u32[]{:S(2)}) copy-start(bf16[192,1024]{1,0:T(8,128)(2,1)} %w1_hbm.1) | copy-start | bytes 1179652
  2.2 1.0 %copy-start.2 = (f32[4,768]{1,0:T(4,128)S(1)}, f32[4,768]{1,0:T(4,128)}, u32[]{:S(2)}) copy-start(f32[4,768]{1,0:T(4,128)} %table_ref.1) | copy-start | bytes 36868
  2.3 1.0 %copy-start.3 = (s32[256]{0:T(256)S(1)}, s32[256]{0:T(256)}, u32[]{:S(2)}) copy-start(s32[256]{0:T(256)} %param.16) | copy-start | bytes 3076
  2.3 1.0 %copy-start.4 = (f32[48]{0:T(128)S(1)}, f32[48]{0:T(128)}, u32[]{:S(2)}) copy-start(f32[48]{0:T(128)} %param.15) | copy-start | bytes 580
  2.3 1.0 %copy-start.5 = (f32[100]{0:T(128)S(1)}, f32[100]{0:T(128)}, u32[]{:S(2)}) copy-start(f32[100]{0:T(128)} %param.17) | copy-start | bytes 1204
  3.3 1.2 %copy-start = (bf16[2,1,1024,256]{3,2,1,0:T(8,128)(2,1)S(1)}, bf16[2,1,1024,256]{3,2,1,0:T(8,128)(2,1)}, u32[]{:S(2)}) copy-start(bf16[2,1,1024,256]{3,2,1,0:T(8,128)(2,1)} %lat_hbm.1) | copy-start | bytes 3145732

commit v2 on v1

v2 whole, which is shorter than its diff:
```python
import functools
import math

import jax
import jax.numpy as jnp
from jax import lax
from jax.experimental import pallas as pl
from jax.experimental.pallas import tpu as pltpu
from jax.sharding import PartitionSpec as P

alpha_fair = 0.95
smooth_width = 0.05
loss_scale = 64.0
grad_shrink = 1.0 / 1024.0


def smooth_abs(diff):
    return jnp.sqrt(diff * diff + smooth_width * smooth_width) - smooth_width


def smooth_sign(diff):
    return diff / jnp.sqrt(diff * diff + smooth_width * smooth_width)


def on_device(latent, targets, w1, w2, noise_table, member_ids, lat_weight, area_index, var_weight):
    members = lax.axis_size("member")
    grid_count = lax.axis_size("grid")
    inputs = latent[:, 0]
    steps = inputs.shape[0]
    points = inputs.shape[2]
    variables = targets.shape[1]
    total_points = points * grid_count
    fairness = (1.0 - alpha_fair) / members
    pair_coef = (1.0 - fairness) / (members * (members - 1))
    lookup = (jnp.arange(lat_weight.shape[0])[:, None] == area_index[None, :]).astype(jnp.float32)
    area = jnp.sum(lookup * lat_weight[:, None], axis=0)
    local_area = jnp.sum(area)
    area_total = lax.psum(local_area, "grid")
    chooser = (jnp.arange(noise_table.shape[0]) == member_ids[0]).astype(jnp.float32)
    noise = jnp.sum(noise_table * chooser[:, None], axis=0)
    before = (
        jnp.einsum(
            "hl,slp->shp",
            lax.all_gather(w1, "grid", axis=0, tiled=True),
            inputs,
            preferred_element_type=jnp.float32,
        )
        + noise[None, :, None]
    )
    hidden = jax.nn.gelu(before).astype(jnp.bfloat16)
    w2_full = lax.all_gather(w2, "grid", axis=1, tiled=True)
    fields = jnp.einsum("vh,shp->svp", w2_full, hidden, preferred_element_type=jnp.float32)
    weight = var_weight[:, None] * area[None, :]
    everyone = lax.all_gather(fields[None], "member", axis=0, tiled=True)
    spread = fields[None] - everyone
    pair_loss = jnp.sum(smooth_abs(spread), axis=0)
    pair_grad = jnp.sum(smooth_sign(spread), axis=0)
    error = fields - targets
    term = smooth_abs(error) / members - 0.5 * pair_coef * pair_loss
    loss_local = jnp.sum(weight[None] * term)
    cotangent = (
        loss_scale * weight[None] * (smooth_sign(error) / members - pair_coef * pair_grad)
    ).astype(jnp.bfloat16)
    back_hidden = jnp.einsum("vh,svp->shp", w2_full, cotangent, preferred_element_type=jnp.float32)
    unused, pullback = jax.vjp(jax.nn.gelu, before)
    back_before = pullback(back_hidden)[0].astype(jnp.bfloat16)
    back_input = jnp.einsum(
        "hl,shp->slp",
        lax.all_gather(w1, "grid", axis=0, tiled=True),
        back_before,
        preferred_element_type=jnp.float32,
    )
    grad_first = jnp.einsum("shp,slp->hl", back_before, inputs, preferred_element_type=jnp.float32)
    grad_second = jnp.einsum("shp,svp->hv", hidden, cotangent, preferred_element_type=jnp.float32)
    grid_sums = (
        lax.psum_scatter(grad_first, "grid", scatter_dimension=0, tiled=True),
        lax.psum_scatter(grad_second, "grid", scatter_dimension=0, tiled=True),
    )
    first_rows, second_rows = lax.psum((grid_sums[0], grid_sums[1]), "member")
    loss_total = lax.psum(loss_local, ("grid", "member"))
    scale = total_points / area_total
    latent_grad = (back_input * scale).astype(jnp.bfloat16)[:, None]
    w1_grad = first_rows * (scale * grad_shrink)
    w2_grad = jnp.transpose(second_rows) * (scale * grad_shrink)
    loss = jnp.reshape(loss_total / (area_total * steps * variables), (1,))
    return (loss, latent_grad, w1_grad, w2_grad)


MESH = pl.DeviceIdType.MESH
GRID = 4
MEMB = 4
TANH_SCALE = math.sqrt(2.0 / math.pi)
CUBIC = 0.044715


def gelu_and_slope(x):
    square = x * x
    t = jnp.tanh(TANH_SCALE * x * (1.0 + CUBIC * square))
    half = 0.5 * (1.0 + t)
    slope = half + 0.5 * x * (1.0 - t * t) * (TANH_SCALE * (1.0 + 3.0 * CUBIC * square))
    return x * half, slope


def pick(index, values):
    result = values[-1]
    for i in range(len(values) - 1):
        result = jnp.where(index == i, values[i], result)
    return result


def dot(a, b, contract):
    return lax.dot_general(a, b, ((contract[:1], contract[1:]), ((), ())), preferred_element_type=jnp.float32)


class Slots:
    def __init__(self):
        self.count = 0

    def take(self, n=1):
        self.count += n
        return self.count - n


SEM = Slots()
AREA, W_Z = SEM.take(4), SEM.take(4)
W_PLANE, W_CORE = SEM.take(3 * 4), SEM.take(4 * 4)
F_CORE, F_X, F_DIAG = SEM.take(2), SEM.take(2), SEM.take(2)
G_CORE, G_X, G_Z = SEM.take(4), SEM.take(4), SEM.take(4)
G_ENDX, G_ENDC, G_ENDD = SEM.take(1), SEM.take(1), SEM.take(1)
L_MEM, L_GRID = SEM.take(4), SEM.take(4)
QUART = 4
EXTRA = 16


def fused(
    lat_hbm, tgt_hbm, w1_hbm, w2_ref, table_ref, ids_ref, latw_ref, aidx_ref, vw_ref,
    loss_ref, lg_hbm, w1g_hbm, w2g_ref,
    lat, tgt, wx, noise, slope, hid, fall, cot, bb, gbuf, acc, csend, crecv, xs, xr, zs, zr, fin, finf, lgv, pad,
    abuf, lmem, lgrid, ss, rs, ls,
):
    y, g, m = lax.axis_index("rep"), lax.axis_index("grid"), lax.axis_index("member")
    c = lax.rem(m, 2)
    x = lax.div(m, 2)
    quarter = 2 * x + y
    core_peer, x_peer = m + 1 - 2 * c, lax.rem(m + 2, 4)
    diag_peer = lax.rem(core_peer + 2, 4)
    steps, _, feats, points = lat_hbm.shape
    variables = tgt_hbm.shape[0]
    rows = w1_hbm.shape[0]
    half = rows // 2
    span = feats // QUART
    fairness = (1.0 - alpha_fair) / MEMB
    pair_coef = (1.0 - fairness) / (MEMB * (MEMB - 1))

    def block(t):
        return pl.ds(pl.multiple_of(t * rows, rows), rows)

    def send(src, dst, s_index, r_index, **where):
        return pltpu.make_async_remote_copy(
            src_ref=src, dst_ref=dst, send_sem=ss.at[s_index], recv_sem=rs.at[r_index],
            device_id={"grid": where.get("grid", g), "member": where.get("member", m), "rep": where.get("rep", y)},
            device_id_type=MESH,
        )

    def first_rows(o):
        own = wx[pl.ds(o, 1)][0]
        return jnp.concatenate(
            [jnp.concatenate([own[q, i, :half] for q in range(QUART)], axis=1) for i in range(2)], axis=0
        )

    def second_columns(o):
        own = wx[pl.ds(o, 1)][0]
        return jnp.concatenate([own[q, i, half:] for q in range(QUART) for i in range(2)], axis=0)[:, :rows]

    w1_in = [
        pltpu.make_async_copy(
            w1_hbm.at[pl.ds(i * half, half), pl.ds(q * span, span)], wx.at[g, q, i, pl.ds(0, half)], ls.at[8 + 2 * q + i]
        )
        for q in range(QUART)
        for i in range(2)
    ]
    for copy in w1_in:
        copy.start()
    lat_in = pltpu.make_async_copy(lat_hbm.at[:, 0], lat, ls.at[1])
    lat_in.start()
    tgt_in = [pltpu.make_async_copy(tgt_hbm.at[:, s], tgt.at[s], ls.at[5 + s]) for s in range(steps)]
    for copy in tgt_in:
        copy.start()

    barrier = pltpu.get_barrier_semaphore()

    def greet(**where):
        pl.semaphore_signal(
            barrier, inc=1, device_id_type=MESH,
            device_id={"grid": where.get("grid", g), "member": where.get("member", m), "rep": where.get("rep", y)},
        )

    for k in range(1, 4):
        greet(grid=lax.rem(g + k, 4))
        greet(member=lax.rem(m + k, 4))
    greet(rep=1 - y)
    greet(rep=1 - y, member=x_peer)

    pad[...] = jnp.zeros_like(pad)
    pad[:rows, :variables] = w2_ref[...].astype(jnp.float32)
    second = jnp.transpose(pad[...]).astype(jnp.bfloat16)
    for q in range(QUART):
        for i in range(2):
            at = (2 * q + i) * EXTRA
            wx[pl.ds(g, 1), q, i, half:] = second[None, at : at + EXTRA]
    for copy in w1_in:
        copy.wait()
    pl.semaphore_wait(barrier, 8)

    piece = wx.at[g, quarter, c]
    w_sends = [send(piece, piece, W_Z + k, W_Z + g, grid=lax.rem(g + k, 4)) for k in range(1, 4)]
    for copy in w_sends:
        copy.start()

    n_lat = latw_ref.shape[1]
    diagonal = lax.broadcasted_iota(jnp.int32, (n_lat, n_lat), 0) == lax.broadcasted_iota(jnp.int32, (n_lat, n_lat), 1)
    lat_col = jnp.sum(jnp.where(diagonal, latw_ref[...], 0.0), axis=1, keepdims=True)
    lookup = lax.broadcasted_iota(jnp.int32, (n_lat, points), 0) == aidx_ref[...]
    area = jnp.sum(jnp.where(lookup, lat_col, 0.0), axis=0, keepdims=True)
    abuf[pl.ds(g, 1)] = jnp.full((1, 8, 128), jnp.sum(area), jnp.float32)
    area_sends = [
        send(abuf.at[g], abuf.at[g], AREA + k, AREA + g, grid=lax.rem(g + k, 4)) for k in range(1, 4)
    ]
    for copy in area_sends:
        copy.start()
    diagonal = lax.broadcasted_iota(jnp.int32, (variables, variables), 0) == lax.broadcasted_iota(jnp.int32, (variables, variables), 1)
    var_col = jnp.sum(jnp.where(diagonal, vw_ref[...], 0.0), axis=1, keepdims=True)
    weight = var_col * area

    chosen = lax.broadcasted_iota(jnp.int32, table_ref.shape, 0) == ids_ref[0]
    noise_row = jnp.sum(jnp.where(chosen, table_ref[...], 0.0), axis=0, keepdims=True)
    noise[...] = jnp.transpose(jnp.broadcast_to(noise_row, (128, noise_row.shape[1])))
    cot[...] = jnp.zeros_like(cot)
    lat_in.wait()

    fields = [None] * steps
    field_sends = []
    mirrored = g >= 2
    near = jnp.where(mirrored, 3 - g, g)
    owners = []
    for j in range(GRID):
        o = pick(near, (j, (1, 0, 2, 3)[j]))
        owners.append(jnp.where(mirrored, 3 - o, o))
    plane = ((dict(member=x_peer), 2 * (1 - x) + y), (dict(rep=1 - y), 2 * x + 1 - y),
             (dict(member=x_peer, rep=1 - y), 2 * (1 - x) + 1 - y))

    def spread_piece(o):
        mine = wx.at[o, quarter, c]
        send(mine, mine, W_Z + o, W_Z + o).wait_recv()
        for i, (where, _) in enumerate(plane):
            copy = send(mine, mine, W_PLANE + 4 * i + o, W_PLANE + 4 * i + o, **where)
            copy.start()
            w_sends.append(copy)
        copy = send(mine, mine, W_CORE + 12 + o, W_CORE + 12 + o, member=core_peer)
        copy.start()
        w_sends.append(copy)

    def pass_to_core(o):
        for i, (_, q) in enumerate(plane):
            got = wx.at[o, q, c]
            send(got, got, W_PLANE + 4 * i + o, W_PLANE + 4 * i + o).wait_recv()
            copy = send(got, got, W_CORE + 4 * i + o, W_CORE + 4 * i + o, member=core_peer)
            copy.start()
            w_sends.append(copy)

    def have_block(o):
        for i, q in enumerate([q for _, q in plane] + [quarter]):
            got = wx.at[o, q, 1 - c]
            send(got, got, W_CORE + 4 * i + o, W_CORE + 4 * i + o).wait_recv()

    for j in range(GRID):
        o = owners[j]
        if j == 1:
            for later in owners[1:]:
                spread_piece(later)
        if j > 0:
            pass_to_core(o)
            have_block(o)
        shift = noise[block(o), :]
        shift = jnp.concatenate([shift] * (points // 128), axis=1)
        own_first, own_second = first_rows(o), second_columns(o)
        for s in range(steps):
            before = dot(own_first, lat[s], (1, 0)) + shift
            value, grad = gelu_and_slope(before)
            value = value.astype(jnp.bfloat16)
            cols = slice(s * points, (s + 1) * points)
            slope[block(o), cols] = grad
            hid[block(o), cols] = value
            part = dot(own_second, value, (1, 0))
            fields[s] = part if j == 0 else fields[s] + part
            if j == GRID - 1:
                fall[pl.ds(m, 1), s] = fields[s][None, : fall.shape[2]]
                mine = fall.at[m, s]
                pair = (
                    send(mine, mine, F_X + s, F_X + s, member=x_peer),
                    send(mine, mine, F_CORE + s, F_CORE + s, member=core_peer),
                )
                for copy in pair:
                    copy.start()
                field_sends.extend(pair)

    for copy in tgt_in:
        copy.wait()
    for k in range(1, 4):
        o = lax.rem(g + k, 4)
        send(abuf.at[o], abuf.at[o], AREA + k, AREA + o).wait_recv()
    area_total = abuf[0] + abuf[1] + abuf[2] + abuf[3]
    area_total = area_total[:1, :1]
    scale = (points * GRID) / area_total

    for s in range(steps):
        theirs = fall.at[x_peer, s]
        send(theirs, theirs, F_X + s, F_X + s).wait_recv()
        onward = send(theirs, theirs, F_DIAG + s, F_DIAG + s, member=core_peer)
        onward.start()
        field_sends.append(onward)
    loss_sum = jnp.zeros((1, 1), jnp.float32)
    for s in range(steps):
        cols = slice(s * points, (s + 1) * points)
        own = fields[s][:variables]
        error = own - tgt[s]
        root = jnp.sqrt(error * error + smooth_width * smooth_width)
        term = (root - smooth_width) / MEMB
        grad = error / root / MEMB
        near_ref = fall.at[core_peer, s]
        send(near_ref, near_ref, F_CORE + s, F_CORE + s).wait_recv()
        far_ref = fall.at[diag_peer, s]
        for peer in (x_peer, core_peer, diag_peer):
            if peer is diag_peer:
                send(far_ref, far_ref, F_DIAG + s, F_DIAG + s).wait_recv()
            spread = own - fall[pl.ds(peer, 1), s][0, :variables]
            root = jnp.sqrt(spread * spread + smooth_width * smooth_width)
            term = term - (0.5 * pair_coef) * (root - smooth_width)
            grad = grad - pair_coef * (spread / root)
        loss_sum = loss_sum + jnp.sum(weight * term)
        cot[:variables, cols] = (loss_scale * weight * grad).astype(jnp.bfloat16)
        for o in range(GRID):
            hidden_rows = slice(o * rows, (o + 1) * rows)
            back = dot(second_columns(o), cot[:, cols], (0, 0))
            bb[hidden_rows, cols] = (back * slope[hidden_rows, cols]).astype(jnp.bfloat16)

    lmem[pl.ds(m, 1)] = jnp.broadcast_to(loss_sum, (1, 8, 128))
    late = [send(lmem.at[m], lmem.at[m], L_MEM + k, L_MEM + m, member=lax.rem(m + k, 4)) for k in range(1, 4)]
    for copy in late:
        copy.start()

    order = [
        pick(g, (3, 3, 0, 0)),
        pick(g, (2, 0, 3, 1)),
        pick(g, (1, 2, 1, 2)),
        g,
    ]
    fourth = half // 2
    my_half = pl.ds(pl.multiple_of(c * half, half), half)
    their_half = pl.ds(pl.multiple_of((1 - c) * half, half), half)
    my_fourth = pl.ds(pl.multiple_of(x * fourth, fourth), fourth)
    their_fourth = pl.ds(pl.multiple_of((1 - x) * fourth, fourth), fourth)

    def start(copy):
        copy.start()
        late.append(copy)

    def partial(j):
        t = order[j]
        first = dot(bb[block(t), :points], lat[0], (1, 1))
        for s in range(1, steps):
            first = first + dot(bb[block(t), s * points : (s + 1) * points], lat[s], (1, 1))
        gbuf[j, :, :feats] = first
        gbuf[j, :, feats:] = dot(hid[block(t), :], cot[...], (1, 1))
        csend[j] = gbuf[j, their_half].astype(jnp.bfloat16)
        start(send(csend.at[j], crecv.at[j], G_CORE + j, G_CORE + j, member=core_peer))

    def over_x(j):
        send(csend.at[j], crecv.at[j], G_CORE + j, G_CORE + j).wait_recv()
        acc[...] = gbuf[j, my_half] + crecv[j].astype(jnp.float32)
        xs[j] = acc[their_fourth].astype(jnp.bfloat16)
        gbuf[j, :fourth] = acc[my_fourth]
        start(send(xs.at[j], xr.at[j], G_X + j, G_X + j, member=x_peer))

    def along_z(j):
        send(xs.at[j], xr.at[j], G_X + j, G_X + j).wait_recv()
        total = gbuf[j, :fourth] + xr[j].astype(jnp.float32)
        if j == GRID - 1:
            gbuf[j, :fourth] = total
        else:
            zs[j] = total.astype(jnp.bfloat16)
            start(send(zs.at[j], zr.at[g], G_Z + j, G_Z + g, grid=order[j]))

    def back_input(s, q):
        cols = slice(s * points, (s + 1) * points)
        left = jnp.concatenate([wx[o, q, i, :half] for o in range(GRID) for i in range(2)], axis=0)
        lgv[s, q * span : (q + 1) * span] = (dot(left, bb[:, cols], (0, 0)) * scale).astype(jnp.bfloat16)

    pieces = [(s, q) for s in range(steps) for q in range(QUART)]
    for i in range(GRID + 2):
        if i < GRID:
            partial(i)
        if 0 <= i - 1 < GRID:
            over_x(i - 1)
        if i - 2 >= 0:
            along_z(i - 2)
        if i == 2:
            for k in range(1, 4):
                o = lax.rem(m + k, 4)
                send(lmem.at[o], lmem.at[o], L_MEM + k, L_MEM + o).wait_recv()
            lgrid[pl.ds(g, 1)] = (lmem[0] + lmem[1] + lmem[2] + lmem[3])[None]
            for k in range(1, 4):
                start(send(lgrid.at[g], lgrid.at[g], L_GRID + k, L_GRID + g, grid=lax.rem(g + k, 4)))
        if i >= GRID - 1:
            for s, q in pieces[(i - GRID + 1) * 2 : (i - GRID + 2) * 2]:
                back_input(s, q)
    for s, q in pieces[6:]:
        back_input(s, q)
    lg_out = pltpu.make_async_copy(lgv, lg_hbm.at[:, 0], ls.at[3])
    lg_out.start()
    for k in range(1, 4):
        o = lax.rem(g + k, 4)
        send(lgrid.at[o], lgrid.at[o], L_GRID + k, L_GRID + o).wait_recv()
    loss_total = lgrid[0] + lgrid[1] + lgrid[2] + lgrid[3]
    loss_ref[...] = loss_total[:1, :1] / (area_total * (steps * variables))

    total = gbuf[GRID - 1, :fourth]
    for k in range(1, 4):
        o = lax.rem(g + k, 4)
        send(zr.at[o], zr.at[o], G_Z + k, G_Z + o).wait_recv()
        total = total + zr[pl.ds(o, 1)][0].astype(jnp.float32)
    fin[pl.ds(m, 1)] = (total * (scale * grad_shrink)).astype(jnp.bfloat16)[None]

    def give(o, s_index, peer):
        start(send(fin.at[o], fin.at[o], s_index, s_index, member=peer))

    def got(o, s_index):
        send(fin.at[o], fin.at[o], s_index, s_index).wait_recv()

    def finish(o):
        place = 2 * lax.rem(o, 2) + lax.div(o, 2)
        finf[pl.ds(pl.multiple_of(place * fourth, fourth), fourth)] = fin[pl.ds(o, 1)][0].astype(jnp.float32)
        here = pl.ds(pl.multiple_of(place * fourth, fourth), fourth)
        copy = pltpu.make_async_copy(finf.at[here, pl.ds(0, feats)], w1g_hbm.at[here], ls.at[16 + len(outs)])
        copy.start()
        outs.append(copy)

    outs = []
    give(m, G_ENDX, x_peer)
    give(m, G_ENDC, core_peer)
    finish(m)
    got(core_peer, G_ENDC)
    finish(core_peer)
    got(x_peer, G_ENDX)
    give(x_peer, G_ENDD, core_peer)
    finish(x_peer)
    got(diag_peer, G_ENDD)
    finish(diag_peer)
    w2g_ref[...] = finf[:, feats : feats + variables]

    for copy in w_sends + area_sends + field_sends + late:
        copy.wait_send()
    for copy in outs + [lg_out]:
        copy.wait()


def fused_on_device(latent, targets, w1, w2, noise_table, member_ids, lat_weight, area_index, var_weight):
    steps, _, feats, points = latent.shape
    variables = targets.shape[1]
    rows = w1.shape[0]
    hidden = rows * GRID
    half = rows // 2
    wide = feats + 128
    fourth = half // 2
    padded = -(-variables // 8) * 8
    f32, bf16 = jnp.float32, jnp.bfloat16
    hbm, vmem = pl.BlockSpec(memory_space=pl.ANY), pl.BlockSpec(memory_space=pltpu.VMEM)
    smem = pl.BlockSpec(memory_space=pltpu.SMEM)
    loss, latent_grad, w1_grad, w2_grad = pl.pallas_call(
        fused,
        out_shape=(
            jax.ShapeDtypeStruct((1, 1), f32),
            jax.ShapeDtypeStruct(latent.shape, bf16),
            jax.ShapeDtypeStruct((rows, feats), f32),
            jax.ShapeDtypeStruct((rows, variables), f32),
        ),
        in_specs=[hbm, hbm, hbm, vmem, vmem, smem, vmem, vmem, vmem],
        out_specs=(vmem, hbm, hbm, vmem),
        scratch_shapes=[
            pltpu.VMEM((steps, feats, points), bf16),
            pltpu.VMEM((steps, variables, points), f32),
            pltpu.VMEM((GRID, QUART, 2, half + EXTRA, feats // QUART), bf16),
            pltpu.VMEM((hidden, 128), f32),
            pltpu.VMEM((hidden, steps * points), f32),
            pltpu.VMEM((hidden, steps * points), bf16),
            pltpu.VMEM((MEMB, steps, padded, points), f32),
            pltpu.VMEM((128, steps * points), bf16),
            pltpu.VMEM((hidden, steps * points), bf16),
            pltpu.VMEM((GRID, rows, wide), f32),
            pltpu.VMEM((half, wide), f32),
            pltpu.VMEM((GRID, half, wide), bf16),
            pltpu.VMEM((GRID, half, wide), bf16),
            pltpu.VMEM((GRID, fourth, wide), bf16),
            pltpu.VMEM((GRID, fourth, wide), bf16),
            pltpu.VMEM((GRID - 1, fourth, wide), bf16),
            pltpu.VMEM((GRID, fourth, wide), bf16),
            pltpu.VMEM((MEMB, fourth, wide), bf16),
            pltpu.VMEM((rows, wide), f32),
            pltpu.VMEM((steps, feats, points), bf16),
            pltpu.VMEM((256, 128), f32),
            pltpu.VMEM((GRID, 8, 128), f32),
            pltpu.VMEM((MEMB, 8, 128), f32),
            pltpu.VMEM((GRID, 8, 128), f32),
            pltpu.SemaphoreType.DMA((SEM.count,)),
            pltpu.SemaphoreType.DMA((SEM.count,)),
            pltpu.SemaphoreType.DMA((20,)),
        ],
        compiler_params=pltpu.CompilerParams(
            collective_id=0, has_side_effects=True, vmem_limit_bytes=60 * 1024 * 1024
        ),
        cost_estimate=pl.CostEstimate(
            flops=6 * hidden * feats * steps * points, bytes_accessed=4 * 1024 * 1024, transcendentals=hidden * steps * points
        ),
    )(
        latent, jnp.transpose(targets, (1, 0, 2)), w1, jnp.transpose(w2), noise_table, member_ids,
        lat_weight[None, :], area_index[None, :], var_weight[None, :],
    )
    return jnp.reshape(loss, (1,)), latent_grad, w1_grad, jnp.transpose(w2_grad)


def solution(mesh):
    return jax.shard_map(
        on_device if tuple(mesh.shape[a] for a in ("grid", "member")) != (4, 4) else fused_on_device,
        mesh=mesh,
        in_specs=(
            P(None, "member", None, ("rep", "grid")),
            P(None, None, ("rep", "grid")),
            P("grid", None),
            P(None, "grid"),
            P(),
            P(("rep", "member")),
            P(),
            P(("rep", "grid")),
            P(),
        ),
        out_specs=(
            P("rep"),
            P(None, "member", None, ("rep", "grid")),
            P(("rep", "grid"), None),
            P(None, ("rep", "grid")),
        ),
        check_vma=False,
    )
```

time: 73.8 us -> 59.8 us (0.81)
  Pallas kernels: 64.5 us -> 51.9 us
  local copies, waits for them, and re-layouts: 5.73 us -> 3.94 us
    pallas_call x1, Pallas kernels: 64.5 us -> 51.9 us  [fused_on_device(): pl.pallas_call(fused, out_shape=(jax.ShapeDtypeStruct((1, 1), f32), jax.S...]
    unnamed x17 -> x7, local copies, waits for them, and re-layouts: 5.73 us -> 3.94 us
where the time goes in v2:
time: 59.8 us; the launch traced here: 58.9 us
  Pallas kernels  51.9 us (87%)
  local copies, waits for them, and re-layouts  3.94 us (7%)
  between operations  3.05 us (5%)
    pallas_call x1, Pallas kernels, fused_on_device(): pl.pallas_call(fused, out_shape=(jax.ShapeDtypeStruct((1, 1), f32), jax.S...  51.9 us
    unnamed x7, local copies, waits for them, and re-layouts  3.94 us

profile of v2, /device:TPU:0, one launch (start us, length us, event | category | flops | bytes accessed | tf_op | source)
XLA Modules:
  0.0 58.9 jit_solution(14081256646107284440)
XLA Ops:
  1.3 51.9 %shard_map.120 = (f32[1,1]{1,0:T(1,128)}, bf16[2,1,1024,256]{3,2,1,0:T(8,128)(2,1)}, f32[192,1024]{1,0:T(8,128)}, f32[192,100]{1,0:T(8,128)}) custom-call(bf16[2,1,1024,256]{3,2,1,0:T(8,128)(2,1)} %lat_hbm.1, f32[100,2,256]{2,1,0:T(2,128)} %bitcast.8, bf16[192,1024]{1,0:T(8,128)(2,1)} %w1_hbm.1, bf16[192,100]{1,0:T(8,128)(2,1)} %bitcast.9, ...), custom_call_target="tpu_custom_call" | custom-call | flops 2415919104 | bytes 4194304 | tf_op jit(solution)/shard_map/pallas_call | solution.py:479
  53.8 0.0 copy-start
  53.8 2.3 %copy.19 = bf16[2,1,1024,256]{3,2,1,0:T(8,128)(2,1)} copy(bf16[2,1,1024,256]{3,2,1,0:T(8,128)(2,1)} %get-tuple-element.17) | data formatting | bytes 2097152
  56.1 0.0 copy-done
  56.1 0.0 copy-start.1
  56.1 0.9 %copy.20 = f32[192,1024]{1,0:T(8,128)} copy(f32[192,1024]{1,0:T(8,128)S(1)} %copy-done) | data formatting | bytes 1572864
  57.0 0.1 copy-done.1
  57.1 0.6 %copy.21 = f32[100,192]{0,1:T(8,128)} copy(f32[100,192]{0,1:T(8,128)S(1)} %bitcast.7) | data formatting | bytes 153600
Async XLA Ops:
  53.8 2.3 %copy-start = (f32[192,1024]{1,0:T(8,128)S(1)}, f32[192,1024]{1,0:T(8,128)}, u32[]{:S(2)}) copy-start(f32[192,1024]{1,0:T(8,128)} %get-tuple-element.18) | copy-start | bytes 2359300
  56.1 1.0 %copy-start.1 = (f32[192,100]{1,0:T(8,128)S(1)}, f32[192,100]{1,0:T(8,128)}, u32[]{:S(2)}) copy-start(f32[192,100]{1,0:T(8,128)} %get-tuple-element.11) | copy-start | bytes 230404

commit v3 on v2

--- a/solution.py
+++ b/solution.py
@@ -134,8 +134,8 @@
 
 def fused(
     lat_hbm, tgt_hbm, w1_hbm, w2_ref, table_ref, ids_ref, latw_ref, aidx_ref, vw_ref,
-    loss_ref, lg_hbm, w1g_hbm, w2g_ref,
-    lat, tgt, wx, noise, slope, hid, fall, cot, bb, gbuf, acc, csend, crecv, xs, xr, zs, zr, fin, finf, lgv, pad,
+    loss_ref, lg_ref, w1g_ref, w2g_ref,
+    lat, tgt, wx, noise, slope, hid, fall, cot, bb, gbuf, acc, csend, crecv, xs, xr, zs, zr, fin, pad,
     abuf, lmem, lgrid, ss, rs, ls,
 ):
     y, g, m = lax.axis_index("rep"), lax.axis_index("grid"), lax.axis_index("member")
@@ -279,7 +279,8 @@
             for later in owners[1:]:
                 spread_piece(later)
         if j > 0:
-            pass_to_core(o)
+            for later in owners[1:3] if j == 1 else owners[j + 1 : j + 2]:
+                pass_to_core(later)
             have_block(o)
         shift = noise[block(o), :]
         shift = jnp.concatenate([shift] * (points // 128), axis=1)
@@ -313,38 +314,53 @@
     area_total = area_total[:1, :1]
     scale = (points * GRID) / area_total
 
-    for s in range(steps):
+    def relay(s):
         theirs = fall.at[x_peer, s]
         send(theirs, theirs, F_X + s, F_X + s).wait_recv()
         onward = send(theirs, theirs, F_DIAG + s, F_DIAG + s, member=core_peer)
         onward.start()
         field_sends.append(onward)
-    loss_sum = jnp.zeros((1, 1), jnp.float32)
-    for s in range(steps):
+
+    def against_target(s):
+        error = fields[s][:variables] - tgt[s]
+        root = jnp.sqrt(error * error + smooth_width * smooth_width)
+        return (root - smooth_width) / MEMB, error / root / MEMB
+
+    def against(s, peer, term, grad):
+        spread = fields[s][:variables] - fall[pl.ds(peer, 1), s][0, :variables]
+        root = jnp.sqrt(spread * spread + smooth_width * smooth_width)
+        return term - (0.5 * pair_coef) * (root - smooth_width), grad - pair_coef * (spread / root)
+
+    def arrived(s, peer, index):
+        ref = fall.at[peer, s]
+        send(ref, ref, index + s, index + s).wait_recv()
+
+    losses = []
+
+    def backward(s, term, grad):
+        losses.append(jnp.sum(weight * term))
         cols = slice(s * points, (s + 1) * points)
-        own = fields[s][:variables]
-        error = own - tgt[s]
-        root = jnp.sqrt(error * error + smooth_width * smooth_width)
-        term = (root - smooth_width) / MEMB
-        grad = error / root / MEMB
-        near_ref = fall.at[core_peer, s]
-        send(near_ref, near_ref, F_CORE + s, F_CORE + s).wait_recv()
-        far_ref = fall.at[diag_peer, s]
-        for peer in (x_peer, core_peer, diag_peer):
-            if peer is diag_peer:
-                send(far_ref, far_ref, F_DIAG + s, F_DIAG + s).wait_recv()
-            spread = own - fall[pl.ds(peer, 1), s][0, :variables]
-            root = jnp.sqrt(spread * spread + smooth_width * smooth_width)
-            term = term - (0.5 * pair_coef) * (root - smooth_width)
-            grad = grad - pair_coef * (spread / root)
-        loss_sum = loss_sum + jnp.sum(weight * term)
         cot[:variables, cols] = (loss_scale * weight * grad).astype(jnp.bfloat16)
         for o in range(GRID):
             hidden_rows = slice(o * rows, (o + 1) * rows)
             back = dot(second_columns(o), cot[:, cols], (0, 0))
             bb[hidden_rows, cols] = (back * slope[hidden_rows, cols]).astype(jnp.bfloat16)
 
-    lmem[pl.ds(m, 1)] = jnp.broadcast_to(loss_sum, (1, 8, 128))
+    state = []
+    for s in range(steps):
+        term, grad = against_target(s)
+        arrived(s, core_peer, F_CORE)
+        term, grad = against(s, core_peer, term, grad)
+        relay(s)
+        state.append(against(s, x_peer, term, grad))
+        if s > 0:
+            arrived(s - 1, diag_peer, F_DIAG)
+            backward(s - 1, *against(s - 1, diag_peer, *state[s - 1]))
+    arrived(steps - 1, diag_peer, F_DIAG)
+    backward(steps - 1, *against(steps - 1, diag_peer, *state[-1]))
+    loss_sum = sum(losses[1:], losses[0])
+
+    lmem[pl.ds(m, 1)] = jnp.full((1, 8, 128), loss_sum, jnp.float32)
     late = [send(lmem.at[m], lmem.at[m], L_MEM + k, L_MEM + m, member=lax.rem(m + k, 4)) for k in range(1, 4)]
     for copy in late:
         copy.start()
@@ -394,30 +410,27 @@
     def back_input(s, q):
         cols = slice(s * points, (s + 1) * points)
         left = jnp.concatenate([wx[o, q, i, :half] for o in range(GRID) for i in range(2)], axis=0)
-        lgv[s, q * span : (q + 1) * span] = (dot(left, bb[:, cols], (0, 0)) * scale).astype(jnp.bfloat16)
+        lg_ref[s, 0, q * span : (q + 1) * span] = (dot(left, bb[:, cols], (0, 0)) * scale).astype(jnp.bfloat16)
 
     pieces = [(s, q) for s in range(steps) for q in range(QUART)]
-    for i in range(GRID + 2):
+    for i in range(GRID + 1):
         if i < GRID:
             partial(i)
-        if 0 <= i - 1 < GRID:
+        if i > 0:
             over_x(i - 1)
-        if i - 2 >= 0:
-            along_z(i - 2)
-        if i == 2:
+    back_input(*pieces[0])
+    back_input(*pieces[1])
+    for j in range(GRID):
+        along_z(j)
+        if j == 0:
             for k in range(1, 4):
                 o = lax.rem(m + k, 4)
                 send(lmem.at[o], lmem.at[o], L_MEM + k, L_MEM + o).wait_recv()
             lgrid[pl.ds(g, 1)] = (lmem[0] + lmem[1] + lmem[2] + lmem[3])[None]
             for k in range(1, 4):
                 start(send(lgrid.at[g], lgrid.at[g], L_GRID + k, L_GRID + g, grid=lax.rem(g + k, 4)))
-        if i >= GRID - 1:
-            for s, q in pieces[(i - GRID + 1) * 2 : (i - GRID + 2) * 2]:
-                back_input(s, q)
-    for s, q in pieces[6:]:
-        back_input(s, q)
-    lg_out = pltpu.make_async_copy(lgv, lg_hbm.at[:, 0], ls.at[3])
-    lg_out.start()
+        for s, q in pieces[2 + 2 * j : 4 + 2 * j] if j < 3 else []:
+            back_input(s, q)
     for k in range(1, 4):
         o = lax.rem(g + k, 4)
         send(lgrid.at[o], lgrid.at[o], L_GRID + k, L_GRID + o).wait_recv()
@@ -439,13 +452,11 @@
 
     def finish(o):
         place = 2 * lax.rem(o, 2) + lax.div(o, 2)
-        finf[pl.ds(pl.multiple_of(place * fourth, fourth), fourth)] = fin[pl.ds(o, 1)][0].astype(jnp.float32)
         here = pl.ds(pl.multiple_of(place * fourth, fourth), fourth)
-        copy = pltpu.make_async_copy(finf.at[here, pl.ds(0, feats)], w1g_hbm.at[here], ls.at[16 + len(outs)])
-        copy.start()
-        outs.append(copy)
-
-    outs = []
+        value = fin[pl.ds(o, 1)][0].astype(jnp.float32)
+        w1g_ref[here] = value[:, :feats]
+        w2g_ref[here] = value[:, feats : feats + variables]
+
     give(m, G_ENDX, x_peer)
     give(m, G_ENDC, core_peer)
     finish(m)
@@ -456,12 +467,9 @@
     finish(x_peer)
     got(diag_peer, G_ENDD)
     finish(diag_peer)
-    w2g_ref[...] = finf[:, feats : feats + variables]
 
     for copy in w_sends + area_sends + field_sends + late:
         copy.wait_send()
-    for copy in outs + [lg_out]:
-        copy.wait()
 
 
 def fused_on_device(latent, targets, w1, w2, noise_table, member_ids, lat_weight, area_index, var_weight):
@@ -474,18 +482,18 @@
     fourth = half // 2
     padded = -(-variables // 8) * 8
     f32, bf16 = jnp.float32, jnp.bfloat16
-    hbm, vmem = pl.BlockSpec(memory_space=pl.ANY), pl.BlockSpec(memory_space=pltpu.VMEM)
+    hbm, vmem = pl.BlockSpec(memory_space=pltpu.HBM), pl.BlockSpec(memory_space=pltpu.VMEM)
     smem = pl.BlockSpec(memory_space=pltpu.SMEM)
     loss, latent_grad, w1_grad, w2_grad = pl.pallas_call(
         fused,
         out_shape=(
             jax.ShapeDtypeStruct((1, 1), f32),
-            jax.ShapeDtypeStruct(latent.shape, bf16),
-            jax.ShapeDtypeStruct((rows, feats), f32),
-            jax.ShapeDtypeStruct((rows, variables), f32),
+            pltpu.VMEM(latent.shape, bf16),
+            pltpu.VMEM((rows, feats), f32),
+            pltpu.VMEM((rows, variables), f32),
         ),
         in_specs=[hbm, hbm, hbm, vmem, vmem, smem, vmem, vmem, vmem],
-        out_specs=(vmem, hbm, hbm, vmem),
+        out_specs=(vmem, vmem, vmem, vmem),
         scratch_shapes=[
             pltpu.VMEM((steps, feats, points), bf16),
             pltpu.VMEM((steps, variables, points), f32),
@@ -505,15 +513,13 @@
             pltpu.VMEM((GRID - 1, fourth, wide), bf16),
             pltpu.VMEM((GRID, fourth, wide), bf16),
             pltpu.VMEM((MEMB, fourth, wide), bf16),
-            pltpu.VMEM((rows, wide), f32),
-            pltpu.VMEM((steps, feats, points), bf16),
             pltpu.VMEM((256, 128), f32),
             pltpu.VMEM((GRID, 8, 128), f32),
             pltpu.VMEM((MEMB, 8, 128), f32),
             pltpu.VMEM((GRID, 8, 128), f32),
             pltpu.SemaphoreType.DMA((SEM.count,)),
             pltpu.SemaphoreType.DMA((SEM.count,)),
-            pltpu.SemaphoreType.DMA((20,)),
+            pltpu.SemaphoreType.DMA((16,)),
         ],
         compiler_params=pltpu.CompilerParams(
             collective_id=0, has_side_effects=True, vmem_limit_bytes=60 * 1024 * 1024

time: 59.8 us -> 57.2 us (0.957)
  local copies, waits for them, and re-layouts: 3.94 us -> 2.49 us
  Pallas kernels: 51.9 us -> 51.2 us
    unnamed x7 -> x3, local copies, waits for them, and re-layouts: 3.94 us -> 2.49 us
    pallas_call x1, Pallas kernels: 51.9 us -> 51.2 us  [fused_on_device(): pl.pallas_call(fused, out_shape=(jax.ShapeDtypeStruct((1, 1), f32), pltpu...]
where the time goes in v3:
time: 57.2 us; the launch traced here: 56.7 us
  Pallas kernels  51.2 us (90%)
  between operations  2.98 us (5%)
  local copies, waits for them, and re-layouts  2.49 us (4%)
    pallas_call x1, Pallas kernels, fused_on_device(): pl.pallas_call(fused, out_shape=(jax.ShapeDtypeStruct((1, 1), f32), pltpu...  51.2 us
    unnamed x3, local copies, waits for them, and re-layouts  2.49 us

profile of v3, /device:TPU:0, one launch (start us, length us, event | category | flops | bytes accessed | tf_op | source)
XLA Modules:
  0.0 56.7 jit_solution(478139909979423469)
XLA Ops:
  1.3 51.2 %shard_map.120 = (f32[1,1]{1,0:T(1,128)}, bf16[2,1,1024,256]{3,2,1,0:T(8,128)(2,1)S(1)}, f32[192,1024]{1,0:T(8,128)S(1)}, f32[192,100]{1,0:T(8,128)S(1)}) custom-call(bf16[2,1,1024,256]{3,2,1,0:T(8,128)(2,1)} %lat_hbm.1, f32[100,2,256]{2,1,0:T(2,128)} %bitcast.8, bf16[192,1024]{1,0:T(8,128)(2,1)} %w1_hbm.1, bf16[192,100]{1,0:T(8,128)(2,1)} %bitcast.9, ...), custom_call_target="tpu_custom_call" | custom-call | flops 2415919104 | bytes 4194304 | tf_op jit(solution)/shard_map/pallas_call | solution.py:487
  52.5 1.0 %copy.17 = bf16[2,1,1024,256]{3,2,1,0:T(8,128)(2,1)} copy(bf16[2,1,1024,256]{3,2,1,0:T(8,128)(2,1)S(1)} %get-tuple-element.13) | data formatting | bytes 2097152
  53.5 0.6 %copy.19 = f32[100,192]{0,1:T(8,128)} copy(f32[100,192]{0,1:T(8,128)S(1)} %bitcast.7) | data formatting | bytes 153600
  54.1 0.9 %copy.18 = f32[192,1024]{1,0:T(8,128)} copy(f32[192,1024]{1,0:T(8,128)S(1)} %get-tuple-element.14) | data formatting | bytes 1572864

commit v4 on v3

--- a/solution.py
+++ b/solution.py
@@ -323,13 +323,18 @@
 
     def against_target(s):
         error = fields[s][:variables] - tgt[s]
-        root = jnp.sqrt(error * error + smooth_width * smooth_width)
-        return (root - smooth_width) / MEMB, error / root / MEMB
+        square = error * error + smooth_width * smooth_width
+        inverse = lax.rsqrt(square)
+        return (square * inverse - smooth_width) * (1.0 / MEMB), error * inverse * (1.0 / MEMB)
 
     def against(s, peer, term, grad):
         spread = fields[s][:variables] - fall[pl.ds(peer, 1), s][0, :variables]
-        root = jnp.sqrt(spread * spread + smooth_width * smooth_width)
-        return term - (0.5 * pair_coef) * (root - smooth_width), grad - pair_coef * (spread / root)
+        square = spread * spread + smooth_width * smooth_width
+        inverse = lax.rsqrt(square)
+        return (
+            term - (0.5 * pair_coef) * (square * inverse - smooth_width),
+            grad - pair_coef * (spread * inverse),
+        )
 
     def arrived(s, peer, index):
         ref = fall.at[peer, s]

time: 57.2 us -> 57.1 us (level)
  no operation moved by 1% of the time
where the time goes in v4:
time: 57.1 us; the launch traced here: 56.6 us
  Pallas kernels  51.1 us (89%)
  between operations  2.98 us (5%)
  local copies, waits for them, and re-layouts  2.49 us (4%)
    pallas_call x1, Pallas kernels, fused_on_device(): pl.pallas_call(fused, out_shape=(jax.ShapeDtypeStruct((1, 1), f32), pltpu...  51.1 us
    unnamed x3, local copies, waits for them, and re-layouts  2.49 us

profile of v4, /device:TPU:0, one launch (start us, length us, event | category | flops | bytes accessed | tf_op | source)
XLA Modules:
  0.0 56.6 jit_solution(14378361066635966629)
XLA Ops:
  1.3 51.1 %shard_map.120 = (f32[1,1]{1,0:T(1,128)}, bf16[2,1,1024,256]{3,2,1,0:T(8,128)(2,1)S(1)}, f32[192,1024]{1,0:T(8,128)S(1)}, f32[192,100]{1,0:T(8,128)S(1)}) custom-call(bf16[2,1,1024,256]{3,2,1,0:T(8,128)(2,1)} %lat_hbm.1, f32[100,2,256]{2,1,0:T(2,128)} %bitcast.8, bf16[192,1024]{1,0:T(8,128)(2,1)} %w1_hbm.1, bf16[192,100]{1,0:T(8,128)(2,1)} %bitcast.9, ...), custom_call_target="tpu_custom_call" | custom-call | flops 2415919104 | bytes 4194304 | tf_op jit(solution)/shard_map/pallas_call | solution.py:492
  52.4 1.0 %copy.17 = bf16[2,1,1024,256]{3,2,1,0:T(8,128)(2,1)} copy(bf16[2,1,1024,256]{3,2,1,0:T(8,128)(2,1)S(1)} %get-tuple-element.13) | data formatting | bytes 2097152
  53.4 0.6 %copy.19 = f32[100,192]{0,1:T(8,128)} copy(f32[100,192]{0,1:T(8,128)S(1)} %bitcast.7) | data formatting | bytes 153600
  54.0 0.9 %copy.18 = f32[192,1024]{1,0:T(8,128)} copy(f32[192,1024]{1,0:T(8,128)S(1)} %get-tuple-element.14) | data formatting | bytes 1572864
